TPU v7x, 512 devices: a whole 4x4x16 slice. The times are simulated.
512 devices in a mesh: cuts: 32 (over z, x_lo), blk: 16 (over x_hi, y, core).
Axes of the slice: x: 4 (x_hi: 2, x_lo: 2; x = x_hi * 2 + x_lo), y: 4, z: 16, core: 2. Of those that a mesh axis runs over, the one named last changes fastest.
Arguments:
- steps: bfloat16 [512, 2, 512, 512], P(('cuts', 'blk')), as said below
Outputs:
- sidebands: float32 [32, 2, 512, 512], P(None, None, 'blk', 'cuts')
Inputs may be any that keep to these rules, and one draw needn't show every extreme that they name: `steps`: sqrt(512) times every entry lies between -1 and 1.
All inputs are finite; a program needn't handle non-finite values.
Results may differ from a plain program's by a relative error of at most 0.035.
Values may be sent and summed in bfloat16 or wider, within the bound.
A program may use at most 64 MiB of HBM per device.

v0:
```python
import math
import jax
import jax.numpy as jnp
from jax import lax
from jax.sharding import PartitionSpec as P


def from_partner(block, axis, distance):
    count = lax.axis_size(axis)
    route = []
    for low in range(count):
        high = low | 1 << distance
        if high != low and high < count:
            route += [(low, high), (high, low)]
    return lax.ppermute(block, axis, route)


def passed_along(x, axis, by):
    devices = lax.axis_size(axis)
    return lax.ppermute(x, axis, [(i, (i + by) % devices) for i in range(devices)])


def complex_product(left_factor, right_factor):
    real_real = jnp.dot(left_factor[0], right_factor[0], preferred_element_type=jnp.float32)
    imag_imag = jnp.dot(left_factor[1], right_factor[1], preferred_element_type=jnp.float32)
    real_imag = jnp.dot(left_factor[0], right_factor[1], preferred_element_type=jnp.float32)
    imag_real = jnp.dot(left_factor[1], right_factor[0], preferred_element_type=jnp.float32)
    return jnp.stack([real_real - imag_imag, real_imag + imag_real])


def complex_wide(left_factor, right_factor):
    hp = lax.Precision.HIGHEST
    real_real = jnp.dot(left_factor[0], right_factor[0], precision=hp)
    imag_imag = jnp.dot(left_factor[1], right_factor[1], precision=hp)
    real_imag = jnp.dot(left_factor[0], right_factor[1], precision=hp)
    imag_real = jnp.dot(left_factor[1], right_factor[0], precision=hp)
    return jnp.stack([real_real - imag_imag, real_imag + imag_real])


def group_product(left_factor, right_factor):
    if left_factor.dtype == jnp.bfloat16:
        return complex_product(left_factor, right_factor)
    return complex_wide(left_factor, right_factor)


def per_device(steps):
    current = steps[0]
    order = current.shape[-1]
    blk_count = lax.axis_size("blk")
    block_rows = order // blk_count
    tree_depth = blk_count.bit_length() - 1
    blk_index = lax.axis_index("blk")
    first_partner = from_partner(current, "blk", 0)
    for section in range(tree_depth):
        if section == 0:
            partner = first_partner
        else:
            partner = from_partner(current, "blk", section)
        is_upper = blk_index >> section & 1 == 1
        upper_factor = jnp.where(is_upper, current, partner)
        lower_factor = jnp.where(is_upper, partner, current)
        current = group_product(upper_factor, lower_factor)
    current = current.astype(jnp.bfloat16)
    row_block = lax.dynamic_slice_in_dim(current, blk_index * block_rows, block_rows, 1)
    cuts_count = lax.axis_size("cuts")
    loop_depth = cuts_count.bit_length() - 1
    for section in range(loop_depth):
        distance = 1 << section
        ahead = passed_along(row_block, "cuts", -distance)

        def add_rows(running, incoming, offset, ahead=ahead):
            return complex_product(ahead, incoming)

        empty_sum = jnp.zeros(row_block.shape, jnp.float32)
        running = add_rows(
            empty_sum, lax.all_gather(row_block, "blk", axis=1, tiled=True), jnp.int32(0)
        )
        row_block = running.astype(jnp.bfloat16)
    received = lax.all_to_all(row_block[None], "cuts", split_axis=3, concat_axis=0, tiled=True)
    slice_count = received.shape[0]
    freq_index = jnp.arange(slice_count, dtype=jnp.int32)
    phase_angle = (
        2.0
        * math.pi
        / slice_count
        * (freq_index[:, None] * freq_index[None, :] % slice_count).astype(jnp.float32)
    )
    cosine_table = jnp.cos(phase_angle)
    sine_table = jnp.sin(phase_angle)
    flattened = received.astype(jnp.float32).reshape(slice_count, 2, -1)
    hp = lax.Precision.HIGHEST
    real_part = jnp.dot(cosine_table, flattened[:, 0], precision=hp) + jnp.dot(
        sine_table, flattened[:, 1], precision=hp
    )
    imag_part = jnp.dot(cosine_table, flattened[:, 1], precision=hp) - jnp.dot(
        sine_table, flattened[:, 0], precision=hp
    )
    norm_factor = math.sqrt(order / slice_count)
    result = jnp.stack([real_part, imag_part], axis=1) * norm_factor
    return result.reshape(received.shape)


def solution(mesh):
    in_specs = (P(("cuts", "blk"), None, None, None),)
    out_specs = P(None, None, "blk", "cuts")
    return jax.shard_map(
        per_device, mesh=mesh, in_specs=in_specs, out_specs=out_specs, check_vma=False
    )
```

profile of v0, /device:TPU:2, one launch (start us, length us, event | category | flops | bytes accessed | tf_op | source)
XLA Modules:
  0.0 564.4 jit_solution(16650119582925848394)
XLA Ops:
  6.5 1.9 collective-permute-start
  8.5 2.8 collective-permute-done
  11.3 1.4 broadcast_select_fusion.1
  14.4 1.5 pad_maximum_fusion
  15.9 3.5 collective-permute-start.1
  19.4 46.4 %collective-permute-done.1 = f32[2,512,512]{2,1,0:T(8,128)} collective-permute-done((f32[2,512,512]{2,1,0:T(8,128)}, f32[2,512,512]{2,1,0:T(8,128)}, u32[]{:S(2)}, u32[]{:S(2)}) %collective-permute-start.1) | collective-permute-done | bytes 2097184 | tf_op jit(solution)/shard_map/ppermute | solution.py:15
  65.8 2.3 broadcast_select_fusion.3
  68.1 1.8 fusion.31
  70.0 1.8 fusion.30
  71.8 1.8 fusion.3
  73.7 1.8 fusion.2
  75.6 1.5 pad_maximum_fusion.1
  77.1 5.3 collective-permute-start.2
  82.3 45.3 %collective-permute-done.2 = f32[2,512,512]{2,1,0:T(8,128)} collective-permute-done((f32[2,512,512]{2,1,0:T(8,128)}, f32[2,512,512]{2,1,0:T(8,128)}, u32[]{:S(2)}, u32[]{:S(2)}) %collective-permute-start.2) | collective-permute-done | bytes 2097184 | tf_op jit(solution)/shard_map/ppermute | solution.py:15
  127.6 2.3 broadcast_select_fusion.5
  129.9 1.8 fusion.33
  131.8 1.8 fusion.32
  133.7 1.8 fusion.1
  135.5 1.8 fusion
  137.4 1.5 pad_maximum_fusion.2
  138.9 4.2 collective-permute-start.3
  143.1 45.4 %collective-permute-done.3 = f32[2,512,512]{2,1,0:T(8,128)} collective-permute-done((f32[2,512,512]{2,1,0:T(8,128)}, f32[2,512,512]{2,1,0:T(8,128)}, u32[]{:S(2)}, u32[]{:S(2)}) %collective-permute-start.3) | collective-permute-done | bytes 2097184 | tf_op jit(solution)/shard_map/ppermute | solution.py:15
  188.5 2.3 broadcast_select_fusion.6
  190.8 1.9 fusion.34
  192.7 1.9 fusion.35
  194.6 1.9 fusion.8
  196.4 1.9 fusion.9
  199.1 7.8 %collective-permute-start.4 = (bf16[2,32,512]{2,1,0:T(8,128)(2,1)}, bf16[2,32,512]{2,1,0:T(8,128)(2,1)S(1)}, u32[]{:S(2)}, u32[]{:S(2)}) collective-permute-start(bf16[2,32,512]{2,1,0:T(8,128)(2,1)} %fusion.50), channel_id=1, source_target_pairs={{0,496},{16,0},{32,16},{48,32},{64,48},{80,64},{96,80},{112,96},{1... | collective-permute-start | bytes 196616 | tf_op jit(solution)/shard_map/ppermute | solution.py:20
  206.9 2.2 collective-permute-done.4
  209.1 53.8 %all-gather.6.cloned.1.call-done = bf16[2,512,512]{2,1,0:T(8,128)(2,1)} async-done(((bf16[2,32,512]{2,1,0:T(8,128)(2,1)}), bf16[2,512,512]{2,1,0:T(8,128)(2,1)}) %all-gather.6.cloned.1.call-update) | async-done | bytes 1048592 | tf_op jit(solution)/shard_map/all_gather | solution.py:76
  268.6 6.0 %collective-permute-start.5 = (bf16[2,32,512]{2,1,0:T(8,128)(2,1)}, bf16[2,32,512]{2,1,0:T(8,128)(2,1)S(1)}, u32[]{:S(2)}, u32[]{:S(2)}) collective-permute-start(bf16[2,32,512]{2,1,0:T(8,128)(2,1)} %pad_maximum_fusion.3), channel_id=1, source_target_pairs={{0,480},{16,496},{32,0},{48,16},{64,32},{80,48},{96,64},{112,80},{... | collective-permute-start | bytes 196616 | tf_op jit(solution)/shard_map/ppermute | solution.py:20
  274.5 2.2 collective-permute-done.5
  276.7 51.0 %all-gather.8.cloned.1.call-done = bf16[2,512,512]{2,1,0:T(8,128)(2,1)} async-done(((bf16[2,32,512]{2,1,0:T(8,128)(2,1)}), bf16[2,512,512]{2,1,0:T(8,128)(2,1)}) %all-gather.8.cloned.1.call-update) | async-done | bytes 1048592 | tf_op jit(solution)/shard_map/all_gather | solution.py:76
  331.4 1.2 fusion.26
  333.3 6.8 %collective-permute-start.6 = (bf16[2,32,512]{2,1,0:T(8,128)(2,1)}, bf16[2,32,512]{2,1,0:T(8,128)(2,1)S(1)}, u32[]{:S(2)}, u32[]{:S(2)}) collective-permute-start(bf16[2,32,512]{2,1,0:T(8,128)(2,1)} %pad_maximum_fusion.4), channel_id=1, source_target_pairs={{0,448},{16,464},{32,480},{48,496},{64,0},{80,16},{96,32},{112,48}... | collective-permute-start | bytes 196616 | tf_op jit(solution)/shard_map/ppermute | solution.py:20
  340.1 3.5 collective-permute-done.6
  343.6 48.8 %all-gather.10.cloned.1.call-done = bf16[2,512,512]{2,1,0:T(8,128)(2,1)} async-done(((bf16[2,32,512]{2,1,0:T(8,128)(2,1)}), bf16[2,512,512]{2,1,0:T(8,128)(2,1)}) %all-gather.10.cloned.1.call-update) | async-done | bytes 1048592 | tf_op jit(solution)/shard_map/all_gather | solution.py:76
  396.2 1.2 fusion.24
  398.1 8.4 %collective-permute-start.7 = (bf16[2,32,512]{2,1,0:T(8,128)(2,1)}, bf16[2,32,512]{2,1,0:T(8,128)(2,1)S(1)}, u32[]{:S(2)}, u32[]{:S(2)}) collective-permute-start(bf16[2,32,512]{2,1,0:T(8,128)(2,1)} %pad_maximum_fusion.5), channel_id=1, source_target_pairs={{0,384},{16,400},{32,416},{48,432},{64,448},{80,464},{96,480},{112... | collective-permute-start | bytes 196616 | tf_op jit(solution)/shard_map/ppermute | solution.py:20
  406.5 6.3 %collective-permute-done.7 = bf16[2,32,512]{2,1,0:T(8,128)(2,1)S(1)} collective-permute-done((bf16[2,32,512]{2,1,0:T(8,128)(2,1)}, bf16[2,32,512]{2,1,0:T(8,128)(2,1)S(1)}, u32[]{:S(2)}, u32[]{:S(2)}) %collective-permute-start.7) | collective-permute-done | bytes 65568 | tf_op jit(solution)/shard_map/ppermute | solution.py:20
  412.8 44.4 %all-gather.12.cloned.1.call-done = bf16[2,512,512]{2,1,0:T(8,128)(2,1)} async-done(((bf16[2,32,512]{2,1,0:T(8,128)(2,1)}), bf16[2,512,512]{2,1,0:T(8,128)(2,1)}) %all-gather.12.cloned.1.call-update) | async-done | bytes 1048592 | tf_op jit(solution)/shard_map/all_gather | solution.py:76
  459.7 1.2 fusion.23
  462.9 12.8 %collective-permute-start.8 = (bf16[2,32,512]{2,1,0:T(8,128)(2,1)}, bf16[2,32,512]{2,1,0:T(8,128)(2,1)S(1)}, u32[]{:S(2)}, u32[]{:S(2)}) collective-permute-start(bf16[2,32,512]{2,1,0:T(8,128)(2,1)} %pad_maximum_fusion.6), channel_id=1, source_target_pairs={{0,256},{16,272},{32,288},{48,304},{64,320},{80,336},{96,352},{112... | collective-permute-start | bytes 196616 | tf_op jit(solution)/shard_map/ppermute | solution.py:20
  475.7 3.0 collective-permute-done.8
  478.7 43.3 %all-gather.14.cloned.1.call-done = bf16[2,512,512]{2,1,0:T(8,128)(2,1)} async-done(((bf16[2,32,512]{2,1,0:T(8,128)(2,1)}), bf16[2,512,512]{2,1,0:T(8,128)(2,1)}) %all-gather.14.cloned.1.call-update) | async-done | bytes 1048592 | tf_op jit(solution)/shard_map/all_gather | solution.py:76
  524.5 1.2 fusion.21
  527.4 27.2 %all_to_all.15 = bf16[32,2,512]{2,1,0:T(2,128)(2,1)S(1)} all-to-all(bf16[32,2,512]{2,1,0:T(2,128)(2,1)S(1)} %reshape.43), channel_id=1, replica_groups=mesh['cuts'=32,'blk'=16] {'cuts'}, dimensions={0} | all-to-all | bytes 131072 | tf_op jit(solution)/shard_map/all_to_all | solution.py:79
  556.6 1.3 copy.18
  (48 shorter events, 27.3 us)
Async XLA Ops:
  6.5 256.4 %all-gather.6.cloned.1.call-start = ((), (), s32[]{:S(2)}) async-start(), calls=%async_computation.1 | async-start | bytes 1114112 | tf_op jit(solution)/shard_map/all_gather | solution.py:76
  6.5 4.8 collective-permute-start
  15.9 49.9 %collective-permute-start.1 = (f32[2,512,512]{2,1,0:T(8,128)}, f32[2,512,512]{2,1,0:T(8,128)}, u32[]{:S(2)}, u32[]{:S(2)}) collective-permute-start(f32[2,512,512]{2,1,0:T(8,128)} %pad_maximum_fusion), channel_id=1, source_target_pairs={{0,2},{2,0},{1,3},{3,1},{4,6},{6,4},{5,7},{7,5},{8,10},{10,8},{9,1... | collective-permute-start | bytes 6291464 | tf_op jit(solution)/shard_map/ppermute | solution.py:15
  77.1 50.5 %collective-permute-start.2 = (f32[2,512,512]{2,1,0:T(8,128)}, f32[2,512,512]{2,1,0:T(8,128)}, u32[]{:S(2)}, u32[]{:S(2)}) collective-permute-start(f32[2,512,512]{2,1,0:T(8,128)} %pad_maximum_fusion.1), channel_id=1, source_target_pairs={{0,4},{4,0},{1,5},{5,1},{2,6},{6,2},{3,7},{7,3},{8,12},{12,8},{9,1... | collective-permute-start | bytes 6291464 | tf_op jit(solution)/shard_map/ppermute | solution.py:15
  138.9 49.6 %collective-permute-start.3 = (f32[2,512,512]{2,1,0:T(8,128)}, f32[2,512,512]{2,1,0:T(8,128)}, u32[]{:S(2)}, u32[]{:S(2)}) collective-permute-start(f32[2,512,512]{2,1,0:T(8,128)} %pad_maximum_fusion.2), channel_id=1, source_target_pairs={{0,8},{8,0},{1,9},{9,1},{2,10},{10,2},{3,11},{11,3},{4,12},{12,4},... | collective-permute-start | bytes 6291464 | tf_op jit(solution)/shard_map/ppermute | solution.py:15
  199.0 128.7 %all-gather.8.cloned.1.call-start = ((), (), s32[]{:S(2)}) async-start(), calls=%async_computation.2 | async-start | bytes 1114112 | tf_op jit(solution)/shard_map/all_gather | solution.py:76
  199.1 10.0 %collective-permute-start.4 = (bf16[2,32,512]{2,1,0:T(8,128)(2,1)}, bf16[2,32,512]{2,1,0:T(8,128)(2,1)S(1)}, u32[]{:S(2)}, u32[]{:S(2)}) collective-permute-start(bf16[2,32,512]{2,1,0:T(8,128)(2,1)} %fusion.50), channel_id=1, source_target_pairs={{0,496},{16,0},{32,16},{48,32},{64,48},{80,64},{96,80},{112,96},{1... | collective-permute-start | bytes 196616 | tf_op jit(solution)/shard_map/ppermute | solution.py:20
  268.5 123.9 %all-gather.10.cloned.1.call-start = ((), (), s32[]{:S(2)}) async-start(), calls=%async_computation.3 | async-start | bytes 1114112 | tf_op jit(solution)/shard_map/all_gather | solution.py:76
  268.6 8.2 %collective-permute-start.5 = (bf16[2,32,512]{2,1,0:T(8,128)(2,1)}, bf16[2,32,512]{2,1,0:T(8,128)(2,1)S(1)}, u32[]{:S(2)}, u32[]{:S(2)}) collective-permute-start(bf16[2,32,512]{2,1,0:T(8,128)(2,1)} %pad_maximum_fusion.3), channel_id=1, source_target_pairs={{0,480},{16,496},{32,0},{48,16},{64,32},{80,48},{96,64},{112,80},{... | collective-permute-start | bytes 196616 | tf_op jit(solution)/shard_map/ppermute | solution.py:20
  333.3 123.9 %all-gather.12.cloned.1.call-start = ((), (), s32[]{:S(2)}) async-start(), calls=%async_computation.4 | async-start | bytes 1114112 | tf_op jit(solution)/shard_map/all_gather | solution.py:76
  333.3 10.3 %collective-permute-start.6 = (bf16[2,32,512]{2,1,0:T(8,128)(2,1)}, bf16[2,32,512]{2,1,0:T(8,128)(2,1)S(1)}, u32[]{:S(2)}, u32[]{:S(2)}) collective-permute-start(bf16[2,32,512]{2,1,0:T(8,128)(2,1)} %pad_maximum_fusion.4), channel_id=1, source_target_pairs={{0,448},{16,464},{32,480},{48,496},{64,0},{80,16},{96,32},{112,48}... | collective-permute-start | bytes 196616 | tf_op jit(solution)/shard_map/ppermute | solution.py:20
  398.1 123.9 %all-gather.14.cloned.1.call-start = ((), (), s32[]{:S(2)}) async-start(), calls=%async_computation.5 | async-start | bytes 1114112 | tf_op jit(solution)/shard_map/all_gather | solution.py:76
  398.1 14.7 %collective-permute-start.7 = (bf16[2,32,512]{2,1,0:T(8,128)(2,1)}, bf16[2,32,512]{2,1,0:T(8,128)(2,1)S(1)}, u32[]{:S(2)}, u32[]{:S(2)}) collective-permute-start(bf16[2,32,512]{2,1,0:T(8,128)(2,1)} %pad_maximum_fusion.5), channel_id=1, source_target_pairs={{0,384},{16,400},{32,416},{48,432},{64,448},{80,464},{96,480},{112... | collective-permute-start | bytes 196616 | tf_op jit(solution)/shard_map/ppermute | solution.py:20
  462.9 15.8 %collective-permute-start.8 = (bf16[2,32,512]{2,1,0:T(8,128)(2,1)}, bf16[2,32,512]{2,1,0:T(8,128)(2,1)S(1)}, u32[]{:S(2)}, u32[]{:S(2)}) collective-permute-start(bf16[2,32,512]{2,1,0:T(8,128)(2,1)} %pad_maximum_fusion.6), channel_id=1, source_target_pairs={{0,256},{16,272},{32,288},{48,304},{64,320},{80,336},{96,352},{112... | collective-permute-start | bytes 196616 | tf_op jit(solution)/shard_map/ppermute | solution.py:20
Sparse Core Ops, SparseCore 0:
  199.1 63.7 all-gather.5
  268.6 58.9 all-gather.7
  333.4 58.9 all-gather.9
  398.2 58.9 all-gather.11
  463.0 58.9 all-gather.13
where the time goes:
time: 566 us; the launch traced here: 564 us
  waiting for transfers between devices  398 us (70%)
  starting transfers between devices  56.8 us (10%)
  matrix products  49.7 us (9%)
  blocking collectives  27.2 us (5%)
  other arithmetic  16.2 us (3%)
  between operations  13.5 us (2%)
    all_gather x5, waiting for transfers between devices, per_device(): lax.all_gather(row_block, 'blk', axis=1, tiled=True)  241 us
    ppermute x4, waiting for transfers between devices, from_partner(): return lax.ppermute(block, axis, route)  140 us
    ppermute x5, starting transfers between devices, passed_along(): lax.ppermute(x, axis, [(i, (i + by) % devices) for i in range(devices)])  41.7 us
    all_to_all x1, blocking collectives, per_device(): lax.all_to_all(row_block[None], 'cuts', split_axis=3, concat_axis=0, tile...  27.2 us
    ppermute x5, waiting for transfers between devices, passed_along(): lax.ppermute(x, axis, [(i, (i + by) % devices) for i in range(devices)])  17.3 us
    ppermute x4, starting transfers between devices, from_partner(): return lax.ppermute(block, axis, route)  14.9 us
  transfers between devices with their start and end apart: 14, of which 14 were waited for; matrix products, arithmetic and copies ran while one was open for 0% of the time, Pallas kernels for 0%

commit v1 on v0

--- a/solution.py
+++ b/solution.py
@@ -73,7 +73,11 @@
 
         empty_sum = jnp.zeros(row_block.shape, jnp.float32)
         running = add_rows(
-            empty_sum, lax.all_gather(row_block, "blk", axis=1, tiled=True), jnp.int32(0)
+            empty_sum,
+            jnp.concatenate(
+                lax.all_to_all(jnp.stack([row_block] * lax.axis_size("blk")), "blk", 0, 0), axis=1
+            ),
+            jnp.int32(0),
         )
         row_block = running.astype(jnp.bfloat16)
     received = lax.all_to_all(row_block[None], "cuts", split_axis=3, concat_axis=0, tiled=True)

time: 566 us -> 350 us (0.62)
  the two profiles are of different devices: /device:TPU:2 before, /device:TPU:6 now
where the time goes in v1:
time: 350 us; the launch traced here: 349 us
  waiting for transfers between devices  168 us (48%)
  starting transfers between devices  101 us (29%)
  blocking collectives  29.2 us (8%)
  matrix products  28.9 us (8%)
  other arithmetic  13 us (4%)
  local copies, waits for them, and re-layouts  8.62 us (2%)
    ppermute x4, waiting for transfers between devices, from_partner(): return lax.ppermute(block, axis, route)  141 us
    ppermute x5, starting transfers between devices, passed_along(): lax.ppermute(x, axis, [(i, (i + by) % devices) for i in range(devices)])  51.9 us
    all_to_all x5, starting transfers between devices, per_device(): lax.all_to_all(jnp.stack([row_block] * lax.axis_size('blk')), 'blk', 0, 0)  34.7 us
    all_to_all x1, blocking collectives, per_device(): lax.all_to_all(row_block[None], 'cuts', split_axis=3, concat_axis=0, tile...  29.2 us
    all_to_all x5, waiting for transfers between devices, per_device(): lax.all_to_all(jnp.stack([row_block] * lax.axis_size('blk')), 'blk', 0, 0)  24.2 us
    ppermute x4, starting transfers between devices, from_partner(): return lax.ppermute(block, axis, route)  14.2 us
  transfers between devices with their start and end apart: 14, of which 10 were waited for; matrix products, arithmetic and copies ran while one was open for 0% of the time, Pallas kernels for 0%

profile of v1, /device:TPU:6, one launch (start us, length us, event | category | flops | bytes accessed | tf_op | source)
XLA Modules:
  0.0 348.7 jit_solution(1214684627302529441)
XLA Ops:
  0.0 1.9 collective-permute-start
  1.9 2.8 collective-permute-done
  4.8 1.4 broadcast_select_fusion.1
  7.9 1.5 pad_maximum_fusion
  9.4 3.5 collective-permute-start.1
  12.9 46.4 %collective-permute-done.1 = f32[2,512,512]{2,1,0:T(8,128)} collective-permute-done((f32[2,512,512]{2,1,0:T(8,128)}, f32[2,512,512]{2,1,0:T(8,128)}, u32[]{:S(2)}, u32[]{:S(2)}) %collective-permute-start.1) | collective-permute-done | bytes 2097184 | tf_op jit(solution)/shard_map/ppermute | solution.py:15
  59.3 2.3 broadcast_select_fusion.3
  61.6 1.8 fusion.31
  63.4 1.8 fusion.30
  65.3 1.9 fusion.3
  67.2 1.8 fusion.2
  69.0 1.5 pad_maximum_fusion.1
  70.5 5.3 %collective-permute-start.2 = (f32[2,512,512]{2,1,0:T(8,128)}, f32[2,512,512]{2,1,0:T(8,128)}, u32[]{:S(2)}, u32[]{:S(2)}) collective-permute-start(f32[2,512,512]{2,1,0:T(8,128)} %pad_maximum_fusion.1), channel_id=1, source_target_pairs={{0,4},{4,0},{1,5},{5,1},{2,6},{6,2},{3,7},{7,3},{8,12},{12,8},{9,1... | collective-permute-start | bytes 6291464 | tf_op jit(solution)/shard_map/ppermute | solution.py:15
  75.8 45.3 %collective-permute-done.2 = f32[2,512,512]{2,1,0:T(8,128)} collective-permute-done((f32[2,512,512]{2,1,0:T(8,128)}, f32[2,512,512]{2,1,0:T(8,128)}, u32[]{:S(2)}, u32[]{:S(2)}) %collective-permute-start.2) | collective-permute-done | bytes 2097184 | tf_op jit(solution)/shard_map/ppermute | solution.py:15
  121.1 2.3 broadcast_select_fusion.5
  123.4 1.9 fusion.33
  125.3 1.8 fusion.32
  127.1 1.8 fusion.1
  129.0 1.8 fusion
  130.8 1.5 pad_maximum_fusion.2
  132.3 3.5 %collective-permute-start.3 = (f32[2,512,512]{2,1,0:T(8,128)}, f32[2,512,512]{2,1,0:T(8,128)}, u32[]{:S(2)}, u32[]{:S(2)}) collective-permute-start(f32[2,512,512]{2,1,0:T(8,128)} %pad_maximum_fusion.2), channel_id=1, source_target_pairs={{0,8},{8,0},{1,9},{9,1},{2,10},{10,2},{3,11},{11,3},{4,12},{12,4},... | collective-permute-start | bytes 6291464 | tf_op jit(solution)/shard_map/ppermute | solution.py:15
  135.9 46.1 %collective-permute-done.3 = f32[2,512,512]{2,1,0:T(8,128)} collective-permute-done((f32[2,512,512]{2,1,0:T(8,128)}, f32[2,512,512]{2,1,0:T(8,128)}, u32[]{:S(2)}, u32[]{:S(2)}) %collective-permute-start.3) | collective-permute-done | bytes 2097184 | tf_op jit(solution)/shard_map/ppermute | solution.py:15
  181.9 2.3 broadcast_select_fusion.6
  184.3 1.9 fusion.34
  186.1 1.9 fusion.35
  188.0 1.9 fusion.8
  189.9 1.9 fusion.9
  191.8 1.1 stack.97
  192.9 7.5 %all-to-all-start = ((bf16[16,2,32,512]{3,2,1,0:T(8,128)(2,1)}), bf16[16,2,32,512]{3,2,1,0:T(8,128)(2,1)S(1)}, u32[]{:S(2)}, u32[]{:S(2)}) async-start(bf16[16,2,32,512]{3,2,1,0:T(8,128)(2,1)} %stack.97), calls=%async_computation | async-start | bytes 2097152 | tf_op jit(solution)/shard_map/all_to_all | solution.py:78
  200.4 4.6 %collective-permute-start.4 = (bf16[2,32,512]{2,1,0:T(8,128)(2,1)S(1)}, bf16[2,32,512]{2,1,0:T(8,128)(2,1)S(1)}, u32[]{:S(2)}, u32[]{:S(2)}) collective-permute-start(bf16[2,32,512]{2,1,0:T(8,128)(2,1)S(1)} %fusion.40), channel_id=1, source_target_pairs={{0,496},{16,0},{32,16},{48,32},{64,48},{80,64},{96,80},{112,96},{1... | collective-permute-start | bytes 196616 | tf_op jit(solution)/shard_map/ppermute | solution.py:20
  205.1 10.9 %all-to-all-done = bf16[16,2,32,512]{3,2,1,0:T(8,128)(2,1)S(1)} async-done(((bf16[16,2,32,512]{3,2,1,0:T(8,128)(2,1)}), bf16[16,2,32,512]{3,2,1,0:T(8,128)(2,1)S(1)}, u32[]{:S(2)}, u32[]{:S(2)}) %all-to-all-start) | async-done | bytes 1048608 | tf_op jit(solution)/shard_map/all_to_all | solution.py:78
  216.9 1.1 stack.101
  218.0 6.5 %all-to-all-start.1 = ((bf16[16,2,32,512]{3,2,1,0:T(8,128)(2,1)}), bf16[16,2,32,512]{3,2,1,0:T(8,128)(2,1)S(1)}, u32[]{:S(2)}, u32[]{:S(2)}) async-start(bf16[16,2,32,512]{3,2,1,0:T(8,128)(2,1)} %stack.101), calls=%async_computation.1 | async-start | bytes 2097152 | tf_op jit(solution)/shard_map/all_to_all | solution.py:78
  224.5 11.4 %collective-permute-start.5 = (bf16[2,32,512]{2,1,0:T(8,128)(2,1)S(1)}, bf16[2,32,512]{2,1,0:T(8,128)(2,1)S(1)}, u32[]{:S(2)}, u32[]{:S(2)}) collective-permute-start(bf16[2,32,512]{2,1,0:T(8,128)(2,1)S(1)} %pad_maximum_fusion.3), channel_id=1, source_target_pairs={{0,480},{16,496},{32,0},{48,16},{64,32},{80,48},{96,64},{112,80},{... | collective-permute-start | bytes 196616 | tf_op jit(solution)/shard_map/ppermute | solution.py:20
  235.9 3.8 %all-to-all-done.1 = bf16[16,2,32,512]{3,2,1,0:T(8,128)(2,1)S(1)} async-done(((bf16[16,2,32,512]{3,2,1,0:T(8,128)(2,1)}), bf16[16,2,32,512]{3,2,1,0:T(8,128)(2,1)S(1)}, u32[]{:S(2)}, u32[]{:S(2)}) %all-to-all-start.1) | async-done | bytes 1048608 | tf_op jit(solution)/shard_map/all_to_all | solution.py:78
  240.6 1.1 stack.105
  241.7 6.5 %all-to-all-start.2 = ((bf16[16,2,32,512]{3,2,1,0:T(8,128)(2,1)}), bf16[16,2,32,512]{3,2,1,0:T(8,128)(2,1)S(1)}, u32[]{:S(2)}, u32[]{:S(2)}) async-start(bf16[16,2,32,512]{3,2,1,0:T(8,128)(2,1)} %stack.105), calls=%async_computation.2 | async-start | bytes 2097152 | tf_op jit(solution)/shard_map/all_to_all | solution.py:78
  248.3 11.8 %collective-permute-start.6 = (bf16[2,32,512]{2,1,0:T(8,128)(2,1)S(1)}, bf16[2,32,512]{2,1,0:T(8,128)(2,1)S(1)}, u32[]{:S(2)}, u32[]{:S(2)}) collective-permute-start(bf16[2,32,512]{2,1,0:T(8,128)(2,1)S(1)} %pad_maximum_fusion.4), channel_id=1, source_target_pairs={{0,448},{16,464},{32,480},{48,496},{64,0},{80,16},{96,32},{112,48}... | collective-permute-start | bytes 196616 | tf_op jit(solution)/shard_map/ppermute | solution.py:20
  260.1 3.3 all-to-all-done.2
  265.5 6.9 %all-to-all-start.3 = ((bf16[16,2,32,512]{3,2,1,0:T(8,128)(2,1)}), bf16[16,2,32,512]{3,2,1,0:T(8,128)(2,1)S(1)}, u32[]{:S(2)}, u32[]{:S(2)}) async-start(bf16[16,2,32,512]{3,2,1,0:T(8,128)(2,1)} %stack.109), calls=%async_computation.3 | async-start | bytes 2097152 | tf_op jit(solution)/shard_map/all_to_all | solution.py:78
  272.4 12.3 %collective-permute-start.7 = (bf16[2,32,512]{2,1,0:T(8,128)(2,1)S(1)}, bf16[2,32,512]{2,1,0:T(8,128)(2,1)S(1)}, u32[]{:S(2)}, u32[]{:S(2)}) collective-permute-start(bf16[2,32,512]{2,1,0:T(8,128)(2,1)S(1)} %pad_maximum_fusion.5), channel_id=1, source_target_pairs={{0,384},{16,400},{32,416},{48,432},{64,448},{80,464},{96,480},{112... | collective-permute-start | bytes 196616 | tf_op jit(solution)/shard_map/ppermute | solution.py:20
  284.8 2.8 all-to-all-done.3
  287.6 3.0 collective-permute-done.7
  292.6 7.3 %all-to-all-start.4 = ((bf16[16,2,32,512]{3,2,1,0:T(8,128)(2,1)}), bf16[16,2,32,512]{3,2,1,0:T(8,128)(2,1)S(1)}, u32[]{:S(2)}, u32[]{:S(2)}) async-start(bf16[16,2,32,512]{3,2,1,0:T(8,128)(2,1)} %stack.113), calls=%async_computation.4 | async-start | bytes 2097152 | tf_op jit(solution)/shard_map/all_to_all | solution.py:78
  299.9 11.7 %collective-permute-start.8 = (bf16[2,32,512]{2,1,0:T(8,128)(2,1)S(1)}, bf16[2,32,512]{2,1,0:T(8,128)(2,1)S(1)}, u32[]{:S(2)}, u32[]{:S(2)}) collective-permute-start(bf16[2,32,512]{2,1,0:T(8,128)(2,1)S(1)} %pad_maximum_fusion.6), channel_id=1, source_target_pairs={{0,256},{16,272},{32,288},{48,304},{64,320},{80,336},{96,352},{112... | collective-permute-start | bytes 196616 | tf_op jit(solution)/shard_map/ppermute | solution.py:20
  311.5 3.4 all-to-all-done.4
  316.3 29.2 %all_to_all.40 = bf16[32,2,512]{2,1,0:T(2,128)(2,1)S(1)} all-to-all(bf16[32,2,512]{2,1,0:T(2,128)(2,1)S(1)} %reshape.126), channel_id=1, replica_groups=mesh['cuts'=32,'blk'=16] {'cuts'}, dimensions={0} | all-to-all | bytes 131072 | tf_op jit(solution)/shard_map/all_to_all | solution.py:83
  347.5 1.3 copy.18
  (53 shorter events, 10.8 us)
Async XLA Ops:
  0.0 4.8 %collective-permute-start = (bf16[2,512,512]{2,1,0:T(8,128)(2,1)}, bf16[2,512,512]{2,1,0:T(8,128)(2,1)S(1)}, u32[]{:S(2)}, u32[]{:S(2)}) collective-permute-start(bf16[2,512,512]{2,1,0:T(8,128)(2,1)} %bitcast.227), channel_id=1, source_target_pairs={{0,1},{1,0},{2,3},{3,2},{4,5},{5,4},{6,7},{7,6},{8,9},{9,8},{10,11... | collective-permute-start | bytes 3145736 | tf_op jit(solution)/shard_map/ppermute | solution.py:15
  9.4 49.9 %collective-permute-start.1 = (f32[2,512,512]{2,1,0:T(8,128)}, f32[2,512,512]{2,1,0:T(8,128)}, u32[]{:S(2)}, u32[]{:S(2)}) collective-permute-start(f32[2,512,512]{2,1,0:T(8,128)} %pad_maximum_fusion), channel_id=1, source_target_pairs={{0,2},{2,0},{1,3},{3,1},{4,6},{6,4},{5,7},{7,5},{8,10},{10,8},{9,1... | collective-permute-start | bytes 6291464 | tf_op jit(solution)/shard_map/ppermute | solution.py:15
  70.5 50.5 %collective-permute-start.2 = (f32[2,512,512]{2,1,0:T(8,128)}, f32[2,512,512]{2,1,0:T(8,128)}, u32[]{:S(2)}, u32[]{:S(2)}) collective-permute-start(f32[2,512,512]{2,1,0:T(8,128)} %pad_maximum_fusion.1), channel_id=1, source_target_pairs={{0,4},{4,0},{1,5},{5,1},{2,6},{6,2},{3,7},{7,3},{8,12},{12,8},{9,1... | collective-permute-start | bytes 6291464 | tf_op jit(solution)/shard_map/ppermute | solution.py:15
  132.3 49.6 %collective-permute-start.3 = (f32[2,512,512]{2,1,0:T(8,128)}, f32[2,512,512]{2,1,0:T(8,128)}, u32[]{:S(2)}, u32[]{:S(2)}) collective-permute-start(f32[2,512,512]{2,1,0:T(8,128)} %pad_maximum_fusion.2), channel_id=1, source_target_pairs={{0,8},{8,0},{1,9},{9,1},{2,10},{10,2},{3,11},{11,3},{4,12},{12,4},... | collective-permute-start | bytes 6291464 | tf_op jit(solution)/shard_map/ppermute | solution.py:15
  192.9 23.0 %all-to-all-start = ((bf16[16,2,32,512]{3,2,1,0:T(8,128)(2,1)}), bf16[16,2,32,512]{3,2,1,0:T(8,128)(2,1)S(1)}, u32[]{:S(2)}, u32[]{:S(2)}) async-start(bf16[16,2,32,512]{3,2,1,0:T(8,128)(2,1)} %stack.97), calls=%async_computation | async-start | bytes 2097152 | tf_op jit(solution)/shard_map/all_to_all | solution.py:78
  200.4 15.7 %collective-permute-start.4 = (bf16[2,32,512]{2,1,0:T(8,128)(2,1)S(1)}, bf16[2,32,512]{2,1,0:T(8,128)(2,1)S(1)}, u32[]{:S(2)}, u32[]{:S(2)}) collective-permute-start(bf16[2,32,512]{2,1,0:T(8,128)(2,1)S(1)} %fusion.40), channel_id=1, source_target_pairs={{0,496},{16,0},{32,16},{48,32},{64,48},{80,64},{96,80},{112,96},{1... | collective-permute-start | bytes 196616 | tf_op jit(solution)/shard_map/ppermute | solution.py:20
  218.0 21.6 %all-to-all-start.1 = ((bf16[16,2,32,512]{3,2,1,0:T(8,128)(2,1)}), bf16[16,2,32,512]{3,2,1,0:T(8,128)(2,1)S(1)}, u32[]{:S(2)}, u32[]{:S(2)}) async-start(bf16[16,2,32,512]{3,2,1,0:T(8,128)(2,1)} %stack.101), calls=%async_computation.1 | async-start | bytes 2097152 | tf_op jit(solution)/shard_map/all_to_all | solution.py:78
  224.5 15.3 %collective-permute-start.5 = (bf16[2,32,512]{2,1,0:T(8,128)(2,1)S(1)}, bf16[2,32,512]{2,1,0:T(8,128)(2,1)S(1)}, u32[]{:S(2)}, u32[]{:S(2)}) collective-permute-start(bf16[2,32,512]{2,1,0:T(8,128)(2,1)S(1)} %pad_maximum_fusion.3), channel_id=1, source_target_pairs={{0,480},{16,496},{32,0},{48,16},{64,32},{80,48},{96,64},{112,80},{... | collective-permute-start | bytes 196616 | tf_op jit(solution)/shard_map/ppermute | solution.py:20
  241.7 21.7 %all-to-all-start.2 = ((bf16[16,2,32,512]{3,2,1,0:T(8,128)(2,1)}), bf16[16,2,32,512]{3,2,1,0:T(8,128)(2,1)S(1)}, u32[]{:S(2)}, u32[]{:S(2)}) async-start(bf16[16,2,32,512]{3,2,1,0:T(8,128)(2,1)} %stack.105), calls=%async_computation.2 | async-start | bytes 2097152 | tf_op jit(solution)/shard_map/all_to_all | solution.py:78
  248.3 15.3 %collective-permute-start.6 = (bf16[2,32,512]{2,1,0:T(8,128)(2,1)S(1)}, bf16[2,32,512]{2,1,0:T(8,128)(2,1)S(1)}, u32[]{:S(2)}, u32[]{:S(2)}) collective-permute-start(bf16[2,32,512]{2,1,0:T(8,128)(2,1)S(1)} %pad_maximum_fusion.4), channel_id=1, source_target_pairs={{0,448},{16,464},{32,480},{48,496},{64,0},{80,16},{96,32},{112,48}... | collective-permute-start | bytes 196616 | tf_op jit(solution)/shard_map/ppermute | solution.py:20
  265.5 22.0 %all-to-all-start.3 = ((bf16[16,2,32,512]{3,2,1,0:T(8,128)(2,1)}), bf16[16,2,32,512]{3,2,1,0:T(8,128)(2,1)S(1)}, u32[]{:S(2)}, u32[]{:S(2)}) async-start(bf16[16,2,32,512]{3,2,1,0:T(8,128)(2,1)} %stack.109), calls=%async_computation.3 | async-start | bytes 2097152 | tf_op jit(solution)/shard_map/all_to_all | solution.py:78
  272.4 18.2 %collective-permute-start.7 = (bf16[2,32,512]{2,1,0:T(8,128)(2,1)S(1)}, bf16[2,32,512]{2,1,0:T(8,128)(2,1)S(1)}, u32[]{:S(2)}, u32[]{:S(2)}) collective-permute-start(bf16[2,32,512]{2,1,0:T(8,128)(2,1)S(1)} %pad_maximum_fusion.5), channel_id=1, source_target_pairs={{0,384},{16,400},{32,416},{48,432},{64,448},{80,464},{96,480},{112... | collective-permute-start | bytes 196616 | tf_op jit(solution)/shard_map/ppermute | solution.py:20
  292.6 22.4 %all-to-all-start.4 = ((bf16[16,2,32,512]{3,2,1,0:T(8,128)(2,1)}), bf16[16,2,32,512]{3,2,1,0:T(8,128)(2,1)S(1)}, u32[]{:S(2)}, u32[]{:S(2)}) async-start(bf16[16,2,32,512]{3,2,1,0:T(8,128)(2,1)} %stack.113), calls=%async_computation.4 | async-start | bytes 2097152 | tf_op jit(solution)/shard_map/all_to_all | solution.py:78
  299.9 15.2 %collective-permute-start.8 = (bf16[2,32,512]{2,1,0:T(8,128)(2,1)S(1)}, bf16[2,32,512]{2,1,0:T(8,128)(2,1)S(1)}, u32[]{:S(2)}, u32[]{:S(2)}) collective-permute-start(bf16[2,32,512]{2,1,0:T(8,128)(2,1)S(1)} %pad_maximum_fusion.6), channel_id=1, source_target_pairs={{0,256},{16,272},{32,288},{48,304},{64,320},{80,336},{96,352},{112... | collective-permute-start | bytes 196616 | tf_op jit(solution)/shard_map/ppermute | solution.py:20
